TPU v7x, 32 devices: a whole 2x2x4 slice. The times are simulated.
32 devices in a mesh: bx: 4 (over y, x), by: 8 (over z, core).
Axes of the slice: x: 2, y: 2, z: 4, core: 2. Of those that a mesh axis runs over, the one named last changes fastest.
Arguments:
- populations: float32 [27, 64, 128, 128], P(None, 'bx', 'by'), as said below
- block_level: int32 [256], replicated, may hold values 0 or 1
- new_slot: int32 [256], P(('bx', 'by')), may hold values from 0 to 255, as said below
Outputs:
- density: float32 [256, 4096], P(('bx', 'by'))
- velocity: float32 [3, 256, 4096], P(None, ('bx', 'by'))
Inputs may be any that keep to these rules, and one draw needn't show every extreme that they name: `populations`: every population is positive. new_slot is a permutation; slot s belongs to device s // 8 in the curve order, which is the order of bx+by. Every block stays at its slot or moves to the next or the previous device in that order; at most one block of a device goes to each of those two devices, and it takes the slot of the block that crosses the same cut the other way. Some cut is crossed in every draw.
All inputs are finite; a program needn't handle non-finite values.
Results may differ from a plain program's by a relative error of at most 0.0003.
Values sent between devices are 32-bit elements; how exact they have to be, the bound alone decides.
A program may use at most 192 MiB of HBM per device.

v0:
```python
import functools
import math

import jax
import jax.numpy as jnp
from jax import lax
from jax.experimental import pallas as pl
from jax.experimental.pallas import tpu as pltpu
from jax.sharding import PartitionSpec as P

MESH = pl.DeviceIdType.MESH
TAU_COARSE = 0.56
TAU_FINE = 0.62
TO_FINE = TAU_FINE / (2.0 * TAU_COARSE)
TO_COARSE = 2.0 * TAU_COARSE / TAU_FINE
SMAGORINSKY = 18.0 * math.sqrt(2.0) * 0.17 * 0.17
WEIGHTS = (8.0 / 27, 2.0 / 27, 1.0 / 54, 1.0 / 216)
DIRECTIONS = [(a, b, e) for a in range(3) for b in range(3) for e in range(3)]
SIDES = [(a, b) for a in (0, 2, 1) for b in (1, 0, 2) if (a, b) != (1, 1)]
HALF = [d for d in DIRECTIONS if d > (1, 1, 1)]
PAD = 8


def opposite(direction):
    return tuple(2 - part for part in direction)


def partial_sums(f):
    ends = {(a, b): f[a, b, 0] + f[a, b, 2] for a in range(3) for b in range(3)}
    whole = {key: ends[key] + f[key + (1,)] for key in ends}
    diff = {(a, b): f[a, b, 2] - f[a, b, 0] for a in range(3) for b in range(3)}
    return ends, whole, diff


def first_moments(f):
    ends, whole, diff = partial_sums(f)
    along_x = [whole[a, 0] + whole[a, 1] + whole[a, 2] for a in range(3)]
    y_low = whole[0, 0] + whole[1, 0] + whole[2, 0]
    y_high = whole[0, 2] + whole[1, 2] + whole[2, 2]
    diff_x = [diff[a, 0] + diff[a, 1] + diff[a, 2] for a in range(3)]
    rho = along_x[0] + along_x[1] + along_x[2]
    momentum = (along_x[2] - along_x[0], y_high - y_low, diff_x[0] + diff_x[1] + diff_x[2])
    stress = (ends, whole, diff, along_x, y_low, y_high, diff_x)
    return rho, momentum, stress


def relax(f, base_time, inactive, factor_of):
    rho, (jx, jy, jz), (ends, whole, diff, along_x, y_low, y_high, diff_x) = first_moments(f)
    pxx = along_x[0] + along_x[2]
    pyy = y_low + y_high
    pzz = ends[0, 0]
    for key in list(ends)[1:]:
        pzz = pzz + ends[key]
    pxy = (whole[2, 2] - whole[2, 0]) - (whole[0, 2] - whole[0, 0])
    pxz = diff_x[2] - diff_x[0]
    pyz = (diff[0, 2] + diff[1, 2] + diff[2, 2]) - (diff[0, 0] + diff[1, 0] + diff[2, 0])
    inv = 1.0 / rho
    ux, uy, uz = jx * inv, jy * inv, jz * inv
    third = rho * (1.0 / 3.0)
    pxx = pxx - third - jx * ux
    pyy = pyy - third - jy * uy
    pzz = pzz - third - jz * uz
    pxy = pxy - jx * uy
    pxz = pxz - jx * uz
    pyz = pyz - jy * uz
    off = pxy * pxy + pxz * pxz + pyz * pyz
    norm = jnp.sqrt(pxx * pxx + pyy * pyy + pzz * pzz + (off + off))
    tau = 0.5 * (base_time + jnp.sqrt(base_time * base_time + SMAGORINSKY * norm * inv))
    keep = 1.0 - 1.0 / tau
    if inactive is not None:
        keep = jnp.where(inactive, 1.0, keep)
    rest = 1.0 - 1.5 * (ux * ux + uy * uy + uz * uz)
    scaled = [rho * w for w in WEIGHTS]
    rests = [s * rest for s in scaled]
    squares = [s * 4.5 for s in scaled]
    linear = [s * 3.0 for s in scaled]
    out = {}

    def emit(d, balance):
        out[d] = balance + (f[d] - balance) * (keep * factor_of(d))

    emit((1, 1, 1), rests[0])
    plane = {}
    for a in (1, 2):
        for b in range(3):
            if a == 1 and b == 1:
                plane[a, b] = None
            elif a == 1:
                plane[a, b] = uy if b == 2 else -uy
            else:
                plane[a, b] = ux if b == 1 else (ux + uy if b == 2 else ux - uy)
    for d in HALF:
        a, b, e = d
        level = sum(part != 1 for part in d)
        flat = plane[a, b]
        if flat is None:
            proj = uz
        elif e == 1:
            proj = flat
        else:
            proj = flat + uz if e == 2 else flat - uz
        even = rests[level] + squares[level] * (proj * proj)
        odd = linear[level] * proj
        emit(d, even + odd)
        emit(opposite(d), even - odd)
    return out


def swap_chunks(value, sub, chunk):
    lanes = value.shape[1]
    width = lanes // 8
    for k in (4, 2, 1):
        sub_bit = (sub & k) != 0
        chunk_bit = (chunk & k) != 0
        down = pltpu.roll(pltpu.roll(value, k, 0), lanes - width * k, 1)
        if k == 4:
            value = jnp.where(sub_bit != chunk_bit, down, value)
        else:
            up = pltpu.roll(pltpu.roll(value, 8 - k, 0), width * k, 1)
            value = jnp.where(
                sub_bit & ~chunk_bit, down, jnp.where(~sub_bit & chunk_bit, up, value)
            )
    return value


def kernel(
    sizes,
    level_ref,
    slot_ref,
    pop_ref,
    density_ref,
    velocity_ref,
    held,
    first,
    second,
    factors,
    leave_next,
    leave_prev,
    come_next,
    come_prev,
    load_sem,
    send_sem,
    recv_sem,
    move_send,
    move_recv,
):
    count_x, count_y, size_x, size_y, size_z, blocks = sizes
    halves = size_y // 8
    index_x = lax.axis_index("bx")
    index_y = lax.axis_index("by")
    near_x = [lax.rem(index_x + count_x + a - 1, count_x) for a in range(3)]
    near_y = [lax.rem(index_y + count_y + b - 1, count_y) for b in range(3)]

    loads = []
    parts = load_sem.shape[0]
    step = size_x // parts
    for part in range(parts):
        piece = pl.ds(part * step, step)
        load = pltpu.make_async_copy(pop_ref.at[:, piece], held.at[:, piece], load_sem.at[part])
        load.start()
        loads.append(load)

    barrier = pltpu.get_barrier_semaphore()
    for a, b in SIDES:
        pl.semaphore_signal(
            barrier, inc=1, device_id=(near_x[a], near_y[b]), device_id_type=MESH
        )

    tile = (8, size_z)
    sub = lax.broadcasted_iota(jnp.int32, tile, 0)
    lane = lax.broadcasted_iota(jnp.int32, tile, 1)
    chunk = lane // (size_z // blocks)

    def spread(values, index):
        result = jnp.full(tile, values[0], jnp.int32)
        for n in range(1, len(values)):
            result = jnp.where(index == n, values[n], result)
        return result

    levels = {}
    for a in range(3):
        for b in range(3):
            begin = (near_x[a] * count_y + near_y[b]) * blocks
            flat = spread([level_ref[begin + n] for n in range(blocks)], chunk)
            for e in range(3):
                levels[a, b, e] = pltpu.roll(flat, (1 - e) % size_z, 1) if e != 1 else flat
    own = levels[1, 1, 1]
    fine = own == 1
    coarse = own != 1
    scale = jnp.where(fine, TO_COARSE, TO_FINE)
    base_time = jnp.where(fine, TAU_FINE, TAU_COARSE)
    for edge in range(3):
        for half in range(halves):
            for a, b, e in DIRECTIONS:
                over = a if a == edge and a != 1 else 1
                other = levels[over, 1, e]
                if b == 0 and half == 0:
                    other = jnp.where(sub == 0, levels[over, 0, e], other)
                if b == 2 and half == halves - 1:
                    other = jnp.where(sub == 7, levels[over, 2, e], other)
                factors[edge, half, 9 * a + 3 * b + e] = jnp.where(other != own, scale, 1.0)

    def factor_at(x, half):
        edge = (x + size_x - 1) // size_x + (x + 1) // size_x

        def factor_of(d):
            return factors[edge, half, 9 * d[0] + 3 * d[1] + d[2]]

        return factor_of

    def put(target, x, half, out):
        for d in DIRECTIONS:
            target[d[0], d[1], d[2], x + 1, pl.ds(PAD + 8 * half, 8), :] = out[d]

    def pulled(source, x, half):
        f = {}
        for a, b, e in DIRECTIONS:
            value = source[a, b, e, x + 2 - a, pl.ds(PAD + 8 * half + 1 - b, 8), :]
            f[a, b, e] = pltpu.roll(value, (e - 1) % size_z, 1) if e != 1 else value
        return f

    def held_at(x, half):
        return {
            (a, b, e): held[9 * a + 3 * b + e, x, pl.ds(8 * half, 8), :] for a, b, e in DIRECTIONS
        }

    def exchange(buffer, turn):
        copies = []
        for n, (a, b) in enumerate(SIDES):
            here_x = {0: 1, 2: size_x}
            there_x = {0: size_x + 1, 2: 0}
            here_y = {0: PAD, 2: PAD + size_y - 1}
            there_y = {0: PAD + size_y, 2: PAD - 1}
            dirs_a = pl.ds(a, 1) if a != 1 else pl.ds(0, 3)
            dirs_b = pl.ds(b, 1) if b != 1 else pl.ds(0, 3)
            from_x = pl.ds(here_x[a], 1) if a != 1 else pl.ds(1, size_x)
            into_x = pl.ds(there_x[a], 1) if a != 1 else pl.ds(1, size_x)
            from_y = pl.ds(here_y[b], 1) if b != 1 else pl.ds(PAD, size_y)
            into_y = pl.ds(there_y[b], 1) if b != 1 else pl.ds(PAD, size_y)
            copy = pltpu.make_async_remote_copy(
                src_ref=buffer.at[dirs_a, dirs_b, :, from_x, from_y, :],
                dst_ref=buffer.at[dirs_a, dirs_b, :, into_x, into_y, :],
                send_sem=send_sem.at[turn, n],
                recv_sem=recv_sem.at[turn, n],
                device_id=(near_x[a], near_y[b]),
                device_id_type=MESH,
            )
            copy.start()
            copies.append(copy)
        return copies

    def first_body(x, carry):
        for half in range(halves):
            put(first, x, half, relax(held_at(x, half), base_time, coarse, factor_at(x, half)))
        return carry

    def second_body(x, carry):
        for half in range(halves):
            kept, moved = held_at(x, half), pulled(first, x, half)
            f = {d: jnp.where(fine, moved[d], kept[d]) for d in DIRECTIONS}
            put(second, x, half, relax(f, base_time, None, factor_at(x, half)))
        return carry

    for part in range(parts):
        loads[part].wait()
        lax.fori_loop(part * step, (part + 1) * step, first_body, 0)

    pl.semaphore_wait(barrier, len(SIDES))
    copies = exchange(first, 0)
    for copy in copies:
        copy.wait()
    lax.fori_loop(0, size_x, second_body, 0)
    copies = exchange(second, 1)
    for copy in copies:
        copy.wait()

    curve = index_x * count_y + index_y
    home = spread([slot_ref[n] // blocks for n in range(blocks)], sub)
    to_next = home == curve + 1
    to_prev = home == curve - 1

    def last_body(x, carry):
        for half in range(halves):
            rho, momentum, _ = first_moments(pulled(second, x, half))
            inv = 1.0 / rho
            at = x * halves + half
            cells = pl.ds(pl.multiple_of(at * size_z, size_z), size_z)
            fields = [rho] + [part * inv for part in momentum]
            for n, field in enumerate(fields):
                field = swap_chunks(field, sub, chunk)
                if n == 0:
                    density_ref[:, cells] = field
                else:
                    velocity_ref[n - 1, :, cells] = field
                for mask, buffer in ((to_next, leave_next), (to_prev, leave_prev)):
                    buffer[n, pl.ds(at, 1), :] = jnp.sum(
                        jnp.where(mask, field, 0.0), axis=0, keepdims=True
                    )
        return carry

    lax.fori_loop(0, size_x, last_body, 0)

    after_x = lax.rem(index_x + (index_y + 1) // count_y, count_x)
    before_x = lax.rem(index_x + count_x - (count_y - index_y) // count_y, count_x)
    moves = []
    for n, (source, target, device) in enumerate(
        (
            (leave_next, come_prev, (after_x, near_y[2])),
            (leave_prev, come_next, (before_x, near_y[0])),
        )
    ):
        copy = pltpu.make_async_remote_copy(
            src_ref=source,
            dst_ref=target,
            send_sem=move_send.at[n],
            recv_sem=move_recv.at[n],
            device_id=device,
            device_id_type=MESH,
        )
        copy.start()
        moves.append(copy)
    for copy in moves:
        copy.wait()

    def place_body(x, carry):
        for half in range(halves):
            at = x * halves + half
            cells = pl.ds(pl.multiple_of(at * size_z, size_z), size_z)
            for n in range(4):
                old = density_ref[:, cells] if n == 0 else velocity_ref[n - 1, :, cells]
                up = jnp.broadcast_to(come_prev[n, pl.ds(at, 1), :], tile)
                down = jnp.broadcast_to(come_next[n, pl.ds(at, 1), :], tile)
                new = jnp.where(to_prev, up, jnp.where(to_next, down, old))
                if n == 0:
                    density_ref[:, cells] = new
                else:
                    velocity_ref[n - 1, :, cells] = new
        return carry

    lax.fori_loop(0, size_x, place_body, 0)


def on_device(populations, block_level, new_slot):
    _, size_x, size_y, size_z = populations.shape
    blocks = new_slot.shape[0]
    sizes = (lax.axis_size("bx"), lax.axis_size("by"), size_x, size_y, size_z, blocks)
    cells = size_x * size_y * size_z // blocks
    tiles = cells // size_z
    padded = pltpu.VMEM((3, 3, 3, size_x + 2, size_y + 2 * PAD, size_z), jnp.float32)
    moving = pltpu.VMEM((4, tiles, size_z), jnp.float32)
    return pl.pallas_call(
        functools.partial(kernel, sizes),
        out_shape=(
            jax.ShapeDtypeStruct((blocks, cells), jnp.float32),
            jax.ShapeDtypeStruct((3, blocks, cells), jnp.float32),
        ),
        in_specs=[
            pl.BlockSpec(memory_space=pltpu.SMEM),
            pl.BlockSpec(memory_space=pltpu.SMEM),
            pl.BlockSpec(memory_space=pl.ANY),
        ],
        out_specs=[pl.BlockSpec(memory_space=pltpu.VMEM)] * 2,
        scratch_shapes=[
            pltpu.VMEM(populations.shape, jnp.float32),
            padded,
            padded,
            pltpu.VMEM((3, size_y // 8, 27, 8, size_z), jnp.float32),
            moving,
            moving,
            moving,
            moving,
            pltpu.SemaphoreType.DMA((4,)),
            pltpu.SemaphoreType.DMA((2, len(SIDES))),
            pltpu.SemaphoreType.DMA((2, len(SIDES))),
            pltpu.SemaphoreType.DMA((2,)),
            pltpu.SemaphoreType.DMA((2,)),
        ],
        compiler_params=pltpu.CompilerParams(
            collective_id=0, has_side_effects=True, vmem_limit_bytes=40 * 1024 * 1024
        ),
    )(block_level, new_slot, populations)


def solution(mesh):
    in_specs = (P(None, "bx", "by", None), P(), P(("bx", "by")))
    out_specs = (P(("bx", "by"), None), P(None, ("bx", "by"), None))
    return jax.shard_map(
        on_device, mesh=mesh, in_specs=in_specs, out_specs=out_specs, check_vma=False
    )
```

profile of v0, /device:TPU:0, one launch (start us, length us, event | category | flops | bytes accessed | tf_op | source)
XLA Modules:
  0.0 37.1 jit_solution(393174647937805497)
XLA Ops:
  0.6 0.0 copy-start
  0.6 2.0 %copy-done = f32[27,16,16,128]{3,2,1,0:T(8,128)S(1)} copy-done((f32[27,16,16,128]{3,2,1,0:T(8,128)S(1)}, f32[27,16,16,128]{3,2,1,0:T(8,128)}, u32[]{:S(2)}) %copy-start) | copy-done | bytes 3538968
  2.6 0.0 copy-start.1
  2.6 0.7 %copy-done.1 = s32[256]{0:T(256)S(1)} copy-done((s32[256]{0:T(256)S(1)}, s32[256]{0:T(256)}, u32[]{:S(2)}) %copy-start.1) | copy-done | bytes 1048
  3.3 0.0 copy-start.2
  3.3 0.7 %copy-done.2 = s32[8]{0:T(128)S(1)} copy-done((s32[8]{0:T(128)S(1)}, s32[8]{0:T(128)}, u32[]{:S(2)}) %copy-start.2) | copy-done | bytes 56
  4.0 31.7 %shard_map.50 = (f32[8,4096]{1,0:T(8,128)S(1)}, f32[3,8,4096]{2,1,0:T(8,128)S(1)}) custom-call(s32[256]{0:T(256)S(1)} %copy-done.1, s32[8]{0:T(128)S(1)} %copy-done.2, f32[27,16,16,128]{3,2,1,0:T(8,128)S(1)} %copy-done), custom_call_target="tpu_custom_call" | custom-call | tf_op jit(solution)/shard_map/pallas_call | solution.py:351
  35.7 0.7 %copy.7 = f32[8,4096]{1,0:T(8,128)} copy(f32[8,4096]{1,0:T(8,128)S(1)} %get-tuple-element.4) | data formatting | bytes 262144
  36.4 0.7 %copy.8 = f32[3,8,4096]{2,1,0:T(8,128)} copy(f32[3,8,4096]{2,1,0:T(8,128)S(1)} %get-tuple-element.5) | data formatting | bytes 786432
Async XLA Ops:
  0.6 2.0 %copy-start = (f32[27,16,16,128]{3,2,1,0:T(8,128)S(1)}, f32[27,16,16,128]{3,2,1,0:T(8,128)}, u32[]{:S(2)}) copy-start(f32[27,16,16,128]{3,2,1,0:T(8,128)} %pop_ref.1) | copy-start | bytes 10616836
  2.6 0.7 %copy-start.1 = (s32[256]{0:T(256)S(1)}, s32[256]{0:T(256)}, u32[]{:S(2)}) copy-start(s32[256]{0:T(256)} %level_ref.1) | copy-start | bytes 3076
  3.3 0.7 %copy-start.2 = (s32[8]{0:T(128)S(1)}, s32[8]{0:T(128)}, u32[]{:S(2)}) copy-start(s32[8]{0:T(128)} %slot_ref.1) | copy-start | bytes 100
where the time goes:
time: 37.3 us; the launch traced here: 37.1 us
  Pallas kernels  31.7 us (85%)
  local copies, waits for them, and re-layouts  4.73 us (13%)
  between operations  0.65 us (2%)
    pallas_call x1, Pallas kernels, on_device(): pl.pallas_call(functools.partial(kernel, sizes), out_shape=(jax.ShapeDtyp...  31.7 us
    unnamed x8, local copies, waits for them, and re-layouts  4.73 us

commit v1 on v0

--- a/solution.py
+++ b/solution.py
@@ -125,11 +125,13 @@
 
 def kernel(
     sizes,
-    level_ref,
-    slot_ref,
+    level_hbm,
+    slot_hbm,
     pop_ref,
     density_ref,
     velocity_ref,
+    level_ref,
+    slot_ref,
     held,
     first,
     second,
@@ -151,14 +153,20 @@
     near_x = [lax.rem(index_x + count_x + a - 1, count_x) for a in range(3)]
     near_y = [lax.rem(index_y + count_y + b - 1, count_y) for b in range(3)]
 
+    middle = size_x // 2
+    pieces = ((0, 1), (size_x - 1, size_x), (1, middle), (middle, size_x - 1))
     loads = []
-    parts = load_sem.shape[0]
-    step = size_x // parts
-    for part in range(parts):
-        piece = pl.ds(part * step, step)
-        load = pltpu.make_async_copy(pop_ref.at[:, piece], held.at[:, piece], load_sem.at[part])
+    for n, (low, high) in enumerate(pieces):
+        piece = pl.ds(low, high - low)
+        load = pltpu.make_async_copy(pop_ref.at[:, piece], held.at[:, piece], load_sem.at[n])
         load.start()
         loads.append(load)
+    tables = [
+        pltpu.make_async_copy(level_hbm, level_ref, load_sem.at[len(pieces)]),
+        pltpu.make_async_copy(slot_hbm, slot_ref, load_sem.at[len(pieces) + 1]),
+    ]
+    for table in tables:
+        table.start()
 
     barrier = pltpu.get_barrier_semaphore()
     for a, b in SIDES:
@@ -177,6 +185,8 @@
             result = jnp.where(index == n, values[n], result)
         return result
 
+    for table in tables:
+        table.wait()
     levels = {}
     for a in range(3):
         for b in range(3):
@@ -224,30 +234,43 @@
             (a, b, e): held[9 * a + 3 * b + e, x, pl.ds(8 * half, 8), :] for a, b, e in DIRECTIONS
         }
 
-    def exchange(buffer, turn):
-        copies = []
-        for n, (a, b) in enumerate(SIDES):
-            here_x = {0: 1, 2: size_x}
-            there_x = {0: size_x + 1, 2: 0}
-            here_y = {0: PAD, 2: PAD + size_y - 1}
-            there_y = {0: PAD + size_y, 2: PAD - 1}
-            dirs_a = pl.ds(a, 1) if a != 1 else pl.ds(0, 3)
-            dirs_b = pl.ds(b, 1) if b != 1 else pl.ds(0, 3)
-            from_x = pl.ds(here_x[a], 1) if a != 1 else pl.ds(1, size_x)
-            into_x = pl.ds(there_x[a], 1) if a != 1 else pl.ds(1, size_x)
-            from_y = pl.ds(here_y[b], 1) if b != 1 else pl.ds(PAD, size_y)
-            into_y = pl.ds(there_y[b], 1) if b != 1 else pl.ds(PAD, size_y)
-            copy = pltpu.make_async_remote_copy(
-                src_ref=buffer.at[dirs_a, dirs_b, :, from_x, from_y, :],
-                dst_ref=buffer.at[dirs_a, dirs_b, :, into_x, into_y, :],
-                send_sem=send_sem.at[turn, n],
-                recv_sem=recv_sem.at[turn, n],
-                device_id=(near_x[a], near_y[b]),
-                device_id_type=MESH,
-            )
-            copy.start()
-            copies.append(copy)
-        return copies
+    def send(buffer, turn, side, part=0):
+        a, b = side
+        here_x = {0: 1, 2: size_x}
+        there_x = {0: size_x + 1, 2: 0}
+        here_y = {0: PAD, 2: PAD + size_y - 1}
+        there_y = {0: PAD + size_y, 2: PAD - 1}
+        dirs_a = pl.ds(a, 1) if a != 1 else pl.ds(0, 3)
+        dirs_b = pl.ds(b, 1) if b != 1 else pl.ds(0, 3)
+        along = pl.ds(1 + part * middle, middle)
+        from_x = pl.ds(here_x[a], 1) if a != 1 else along
+        into_x = pl.ds(there_x[a], 1) if a != 1 else along
+        from_y = pl.ds(here_y[b], 1) if b != 1 else pl.ds(PAD, size_y)
+        into_y = pl.ds(there_y[b], 1) if b != 1 else pl.ds(PAD, size_y)
+        number = SIDES.index(side) if a != 1 else 6 + 2 * part + b // 2
+        copy = pltpu.make_async_remote_copy(
+            src_ref=buffer.at[dirs_a, dirs_b, :, from_x, from_y, :],
+            dst_ref=buffer.at[dirs_a, dirs_b, :, into_x, into_y, :],
+            send_sem=send_sem.at[turn, number],
+            recv_sem=recv_sem.at[turn, number],
+            device_id=(near_x[a], near_y[b]),
+            device_id_type=MESH,
+        )
+        copy.start()
+        return copy
+
+    def send_low(buffer, turn):
+        return [send(buffer, turn, (0, b)) for b in (1, 0, 2)]
+
+    def send_high(buffer, turn):
+        return [send(buffer, turn, (2, b)) for b in (1, 0, 2)]
+
+    def send_part(buffer, turn, part):
+        return [send(buffer, turn, (1, b), part) for b in (0, 2)]
+
+    def arrived(copies):
+        for copy in copies:
+            copy.wait_recv()
 
     def first_body(x, carry):
         for half in range(halves):
@@ -261,18 +284,34 @@
             put(second, x, half, relax(f, base_time, None, factor_at(x, half)))
         return carry
 
-    for part in range(parts):
-        loads[part].wait()
-        lax.fori_loop(part * step, (part + 1) * step, first_body, 0)
-
+    loads[0].wait()
+    lax.fori_loop(0, 1, first_body, 0)
     pl.semaphore_wait(barrier, len(SIDES))
-    copies = exchange(first, 0)
-    for copy in copies:
-        copy.wait()
-    lax.fori_loop(0, size_x, second_body, 0)
-    copies = exchange(second, 1)
-    for copy in copies:
-        copy.wait()
+    low = send_low(first, 0)
+    loads[1].wait()
+    lax.fori_loop(size_x - 1, size_x, first_body, 0)
+    high = send_high(first, 0)
+    loads[2].wait()
+    lax.fori_loop(1, middle, first_body, 0)
+    front = send_part(first, 0, 0)
+    loads[3].wait()
+    lax.fori_loop(middle, size_x - 1, first_body, 0)
+    back = send_part(first, 0, 1)
+    sent = low + high + front + back
+
+    arrived(high + front)
+    lax.fori_loop(0, 1, second_body, 0)
+    next_low = send_low(second, 1)
+    lax.fori_loop(1, middle - 1, second_body, 0)
+    arrived(low + back)
+    lax.fori_loop(size_x - 1, size_x, second_body, 0)
+    high = send_high(second, 1)
+    low = next_low
+    lax.fori_loop(middle - 1, middle, second_body, 0)
+    front = send_part(second, 1, 0)
+    lax.fori_loop(middle, size_x - 1, second_body, 0)
+    back = send_part(second, 1, 1)
+    sent = sent + low + high + front + back
 
     curve = index_x * count_y + index_y
     home = spread([slot_ref[n] // blocks for n in range(blocks)], sub)
@@ -298,29 +337,29 @@
                     )
         return carry
 
-    lax.fori_loop(0, size_x, last_body, 0)
-
     after_x = lax.rem(index_x + (index_y + 1) // count_y, count_x)
     before_x = lax.rem(index_x + count_x - (count_y - index_y) // count_y, count_x)
-    moves = []
-    for n, (source, target, device) in enumerate(
-        (
-            (leave_next, come_prev, (after_x, near_y[2])),
-            (leave_prev, come_next, (before_x, near_y[0])),
-        )
-    ):
-        copy = pltpu.make_async_remote_copy(
-            src_ref=source,
-            dst_ref=target,
-            send_sem=move_send.at[n],
-            recv_sem=move_recv.at[n],
-            device_id=device,
-            device_id_type=MESH,
-        )
-        copy.start()
-        moves.append(copy)
-    for copy in moves:
-        copy.wait()
+
+    def migrate(part):
+        rows = pl.ds(part * middle * halves, middle * halves)
+        copies = []
+        for n, (source, target, device) in enumerate(
+            (
+                (leave_next, come_prev, (after_x, near_y[2])),
+                (leave_prev, come_next, (before_x, near_y[0])),
+            )
+        ):
+            copy = pltpu.make_async_remote_copy(
+                src_ref=source.at[:, rows],
+                dst_ref=target.at[:, rows],
+                send_sem=move_send.at[part, n],
+                recv_sem=move_recv.at[part, n],
+                device_id=device,
+                device_id_type=MESH,
+            )
+            copy.start()
+            copies.append(copy)
+        return copies
 
     def place_body(x, carry):
         for half in range(halves):
@@ -337,7 +376,21 @@
                     velocity_ref[n - 1, :, cells] = new
         return carry
 
-    lax.fori_loop(0, size_x, place_body, 0)
+    arrived(high + front)
+    lax.fori_loop(0, middle - 1, last_body, 0)
+    arrived(back)
+    lax.fori_loop(middle - 1, middle, last_body, 0)
+    early = migrate(0)
+    lax.fori_loop(middle, size_x - 1, last_body, 0)
+    arrived(low)
+    lax.fori_loop(size_x - 1, size_x, last_body, 0)
+    late = migrate(1)
+    arrived(early)
+    lax.fori_loop(0, middle, place_body, 0)
+    arrived(late)
+    lax.fori_loop(middle, size_x, place_body, 0)
+    for copy in sent + early + late:
+        copy.wait_send()
 
 
 def on_device(populations, block_level, new_slot):
@@ -355,12 +408,14 @@
             jax.ShapeDtypeStruct((3, blocks, cells), jnp.float32),
         ),
         in_specs=[
-            pl.BlockSpec(memory_space=pltpu.SMEM),
-            pl.BlockSpec(memory_space=pltpu.SMEM),
-            pl.BlockSpec(memory_space=pl.ANY),
+            pl.BlockSpec(memory_space=pltpu.HBM),
+            pl.BlockSpec(memory_space=pltpu.HBM),
+            pl.BlockSpec(memory_space=pltpu.HBM),
         ],
         out_specs=[pl.BlockSpec(memory_space=pltpu.VMEM)] * 2,
         scratch_shapes=[
+            pltpu.SMEM(block_level.shape, jnp.int32),
+            pltpu.SMEM(new_slot.shape, jnp.int32),
             pltpu.VMEM(populations.shape, jnp.float32),
             padded,
             padded,
@@ -369,14 +424,14 @@
             moving,
             moving,
             moving,
-            pltpu.SemaphoreType.DMA((4,)),
-            pltpu.SemaphoreType.DMA((2, len(SIDES))),
-            pltpu.SemaphoreType.DMA((2, len(SIDES))),
-            pltpu.SemaphoreType.DMA((2,)),
-            pltpu.SemaphoreType.DMA((2,)),
+            pltpu.SemaphoreType.DMA((6,)),
+            pltpu.SemaphoreType.DMA((2, 10)),
+            pltpu.SemaphoreType.DMA((2, 10)),
+            pltpu.SemaphoreType.DMA((2, 2)),
+            pltpu.SemaphoreType.DMA((2, 2)),
         ],
         compiler_params=pltpu.CompilerParams(
-            collective_id=0, has_side_effects=True, vmem_limit_bytes=40 * 1024 * 1024
+            collective_id=0, has_side_effects=True, vmem_limit_bytes=60 * 1024 * 1024
         ),
     )(block_level, new_slot, populations)
 

time: 37.3 us -> 31.7 us (0.85)
  Pallas kernels: 31.7 us -> 27.6 us
  local copies, waits for them, and re-layouts: 4.73 us -> 3.33 us
    pallas_call x1, Pallas kernels: 31.7 us -> 27.6 us  [on_device(): pl.pallas_call(functools.partial(kernel, sizes), out_shape=(jax.ShapeDtyp...]
    unnamed x8 -> x2, local copies, waits for them, and re-layouts: 4.73 us -> 3.33 us
where the time goes in v1:
time: 31.7 us; the launch traced here: 31.6 us
  Pallas kernels  27.6 us (87%)
  local copies, waits for them, and re-layouts  3.33 us (11%)
  between operations  0.64 us (2%)
    pallas_call x1, Pallas kernels, on_device(): pl.pallas_call(functools.partial(kernel, sizes), out_shape=(jax.ShapeDtyp...  27.6 us
    unnamed x2, local copies, waits for them, and re-layouts  3.33 us

profile of v1, /device:TPU:0, one launch (start us, length us, event | category | flops | bytes accessed | tf_op | source)
XLA Modules:
  0.0 31.6 jit_solution(12935422830288731086)
XLA Ops:
  0.6 27.6 %shard_map.50 = (f32[8,4096]{1,0:T(8,128)}, f32[3,8,4096]{2,1,0:T(8,128)}) custom-call(s32[256]{0:T(256)} %level_hbm.1, s32[8]{0:T(128)} %slot_hbm.1, f32[27,16,16,128]{3,2,1,0:T(8,128)} %pop_ref.1), custom_call_target="tpu_custom_call" | custom-call | tf_op jit(solution)/shard_map/pallas_call | solution.py:404
  28.2 1.6 %copy.7 = f32[8,4096]{1,0:T(8,128)} copy(f32[8,4096]{1,0:T(8,128)} %get-tuple-element.4) | data formatting | bytes 262144
  29.8 1.8 %copy.8 = f32[3,8,4096]{2,1,0:T(8,128)} copy(f32[3,8,4096]{2,1,0:T(8,128)} %get-tuple-element.5) | data formatting | bytes 786432

commit v2 on v1

--- a/solution.py
+++ b/solution.py
@@ -44,7 +44,7 @@
     return rho, momentum, stress
 
 
-def relax(f, base_time, inactive, factor_of):
+def relax(f, base_time, inactive, kind_of, factor_of):
     rho, (jx, jy, jz), (ends, whole, diff, along_x, y_low, y_high, diff_x) = first_moments(f)
     pxx = along_x[0] + along_x[2]
     pyy = y_low + y_high
@@ -75,9 +75,13 @@
     squares = [s * 4.5 for s in scaled]
     linear = [s * 3.0 for s in scaled]
     out = {}
+    keeps = {(1, 1, 1): keep}
 
     def emit(d, balance):
-        out[d] = balance + (f[d] - balance) * (keep * factor_of(d))
+        kind = kind_of(d)
+        if kind not in keeps:
+            keeps[kind] = keep * factor_of(kind)
+        out[d] = balance + (f[d] - balance) * keeps[kind]
 
     emit((1, 1, 1), rests[0])
     plane = {}
@@ -128,8 +132,9 @@
     level_hbm,
     slot_hbm,
     pop_ref,
-    density_ref,
-    velocity_ref,
+    fields_ref,
+    come_prev,
+    come_next,
     level_ref,
     slot_ref,
     held,
@@ -138,13 +143,13 @@
     factors,
     leave_next,
     leave_prev,
-    come_next,
-    come_prev,
+    fields,
     load_sem,
     send_sem,
     recv_sem,
     move_send,
     move_recv,
+    write_sem,
 ):
     count_x, count_y, size_x, size_y, size_z, blocks = sizes
     halves = size_y // 8
@@ -199,35 +204,50 @@
     coarse = own != 1
     scale = jnp.where(fine, TO_COARSE, TO_FINE)
     base_time = jnp.where(fine, TAU_FINE, TAU_COARSE)
-    for edge in range(3):
-        for half in range(halves):
-            for a, b, e in DIRECTIONS:
-                over = a if a == edge and a != 1 else 1
-                other = levels[over, 1, e]
-                if b == 0 and half == 0:
-                    other = jnp.where(sub == 0, levels[over, 0, e], other)
-                if b == 2 and half == halves - 1:
-                    other = jnp.where(sub == 7, levels[over, 2, e], other)
-                factors[edge, half, 9 * a + 3 * b + e] = jnp.where(other != own, scale, 1.0)
-
-    def factor_at(x, half):
-        edge = (x + size_x - 1) // size_x + (x + 1) // size_x
-
-        def factor_of(d):
-            return factors[edge, half, 9 * d[0] + 3 * d[1] + d[2]]
-
-        return factor_of
+    for a, b, e in DIRECTIONS:
+        other = levels[a, 1, e]
+        if b == 0:
+            other = jnp.where(sub == 0, levels[a, 0, e], other)
+        if b == 2:
+            other = jnp.where(sub == 7, levels[a, 2, e], other)
+        factors[9 * a + 3 * b + e] = jnp.where(other != own, scale, 1.0)
+
+    def kinds(edge, half):
+        def kind_of(d):
+            a, b, e = d
+            row = b if (b == 0 and half == 0) or (b == 2 and half == halves - 1) else 1
+            return (a if a == edge else 1, row, e)
+
+        return kind_of
+
+    def factor_of(kind):
+        return factors[9 * kind[0] + 3 * kind[1] + kind[2]]
 
     def put(target, x, half, out):
         for d in DIRECTIONS:
             target[d[0], d[1], d[2], x + 1, pl.ds(PAD + 8 * half, 8), :] = out[d]
 
+    def row_at(source, x, half, d):
+        a, b, e = d
+        return source[a, b, e, x + 2 - a, pl.ds(PAD + 8 * half + 1 - b, 8), :]
+
+    def along_z(value, e):
+        return pltpu.roll(value, (e - 1) % size_z, 1) if e != 1 else value
+
     def pulled(source, x, half):
-        f = {}
-        for a, b, e in DIRECTIONS:
-            value = source[a, b, e, x + 2 - a, pl.ds(PAD + 8 * half + 1 - b, 8), :]
-            f[a, b, e] = pltpu.roll(value, (e - 1) % size_z, 1) if e != 1 else value
-        return f
+        return {d: along_z(row_at(source, x, half, d), d[2]) for d in DIRECTIONS}
+
+    def pulled_moments(source, x, half):
+        parts = []
+        for e in range(3):
+            rows = [[row_at(source, x, half, (a, b, e)) for b in range(3)] for a in range(3)]
+            xs = [rows[a][0] + rows[a][1] + rows[a][2] for a in range(3)]
+            low = rows[0][0] + rows[1][0] + rows[2][0]
+            high = rows[0][2] + rows[1][2] + rows[2][2]
+            sums = (xs[0] + xs[1] + xs[2], xs[2] - xs[0], high - low)
+            parts.append([along_z(value, e) for value in sums])
+        rho, jx, jy = (parts[0][n] + parts[1][n] + parts[2][n] for n in range(3))
+        return rho, (jx, jy, parts[2][0] - parts[0][0])
 
     def held_at(x, half):
         return {
@@ -272,70 +292,73 @@
         for copy in copies:
             copy.wait_recv()
 
-    def first_body(x, carry):
-        for half in range(halves):
-            put(first, x, half, relax(held_at(x, half), base_time, coarse, factor_at(x, half)))
-        return carry
-
-    def second_body(x, carry):
-        for half in range(halves):
-            kept, moved = held_at(x, half), pulled(first, x, half)
-            f = {d: jnp.where(fine, moved[d], kept[d]) for d in DIRECTIONS}
-            put(second, x, half, relax(f, base_time, None, factor_at(x, half)))
-        return carry
+    def first_pass(begin, end, edge=1):
+        def body(x, carry):
+            for half in range(halves):
+                out = relax(held_at(x, half), base_time, coarse, kinds(edge, half), factor_of)
+                put(first, x, half, out)
+            return carry
+
+        lax.fori_loop(begin, end, body, 0)
+
+    def second_pass(begin, end, edge=1):
+        def body(x, carry):
+            for half in range(halves):
+                kept, moved = held_at(x, half), pulled(first, x, half)
+                f = {d: jnp.where(fine, moved[d], kept[d]) for d in DIRECTIONS}
+                put(second, x, half, relax(f, base_time, None, kinds(edge, half), factor_of))
+            return carry
+
+        lax.fori_loop(begin, end, body, 0)
 
     loads[0].wait()
-    lax.fori_loop(0, 1, first_body, 0)
+    first_pass(0, 1, 0)
     pl.semaphore_wait(barrier, len(SIDES))
     low = send_low(first, 0)
     loads[1].wait()
-    lax.fori_loop(size_x - 1, size_x, first_body, 0)
+    first_pass(size_x - 1, size_x, 2)
     high = send_high(first, 0)
     loads[2].wait()
-    lax.fori_loop(1, middle, first_body, 0)
+    first_pass(1, middle)
     front = send_part(first, 0, 0)
     loads[3].wait()
-    lax.fori_loop(middle, size_x - 1, first_body, 0)
+    first_pass(middle, size_x - 1)
     back = send_part(first, 0, 1)
     sent = low + high + front + back
 
     arrived(high + front)
-    lax.fori_loop(0, 1, second_body, 0)
+    second_pass(0, 1, 0)
     next_low = send_low(second, 1)
-    lax.fori_loop(1, middle - 1, second_body, 0)
+    second_pass(1, middle - 1)
     arrived(low + back)
-    lax.fori_loop(size_x - 1, size_x, second_body, 0)
+    second_pass(size_x - 1, size_x, 2)
     high = send_high(second, 1)
     low = next_low
-    lax.fori_loop(middle - 1, middle, second_body, 0)
+    second_pass(middle - 1, middle)
     front = send_part(second, 1, 0)
-    lax.fori_loop(middle, size_x - 1, second_body, 0)
+    second_pass(middle, size_x - 1)
     back = send_part(second, 1, 1)
     sent = sent + low + high + front + back
 
-    curve = index_x * count_y + index_y
-    home = spread([slot_ref[n] // blocks for n in range(blocks)], sub)
-    to_next = home == curve + 1
-    to_prev = home == curve - 1
-
-    def last_body(x, carry):
-        for half in range(halves):
-            rho, momentum, _ = first_moments(pulled(second, x, half))
-            inv = 1.0 / rho
-            at = x * halves + half
-            cells = pl.ds(pl.multiple_of(at * size_z, size_z), size_z)
-            fields = [rho] + [part * inv for part in momentum]
-            for n, field in enumerate(fields):
-                field = swap_chunks(field, sub, chunk)
-                if n == 0:
-                    density_ref[:, cells] = field
-                else:
-                    velocity_ref[n - 1, :, cells] = field
-                for mask, buffer in ((to_next, leave_next), (to_prev, leave_prev)):
-                    buffer[n, pl.ds(at, 1), :] = jnp.sum(
-                        jnp.where(mask, field, 0.0), axis=0, keepdims=True
-                    )
-        return carry
+    to_next, to_prev = crossings(slot_ref, index_x * count_y + index_y, blocks, sub)
+
+    def last_pass(begin, end):
+        def body(x, carry):
+            for half in range(halves):
+                rho, momentum = pulled_moments(second, x, half)
+                inv = 1.0 / rho
+                at = x * halves + half
+                cells = pl.ds(pl.multiple_of(at * size_z, size_z), size_z)
+                for n, field in enumerate([rho] + [part * inv for part in momentum]):
+                    field = swap_chunks(field, sub, chunk)
+                    fields[n, :, cells] = field
+                    for mask, buffer in ((to_next, leave_next), (to_prev, leave_prev)):
+                        buffer[n, pl.ds(at, 1), :] = jnp.sum(
+                            jnp.where(mask, field, 0.0), axis=0, keepdims=True
+                        )
+            return carry
+
+        lax.fori_loop(begin, end, body, 0)
 
     after_x = lax.rem(index_x + (index_y + 1) // count_y, count_x)
     before_x = lax.rem(index_x + count_x - (count_y - index_y) // count_y, count_x)
@@ -361,36 +384,59 @@
             copies.append(copy)
         return copies
 
-    def place_body(x, carry):
-        for half in range(halves):
-            at = x * halves + half
-            cells = pl.ds(pl.multiple_of(at * size_z, size_z), size_z)
-            for n in range(4):
-                old = density_ref[:, cells] if n == 0 else velocity_ref[n - 1, :, cells]
-                up = jnp.broadcast_to(come_prev[n, pl.ds(at, 1), :], tile)
-                down = jnp.broadcast_to(come_next[n, pl.ds(at, 1), :], tile)
-                new = jnp.where(to_prev, up, jnp.where(to_next, down, old))
-                if n == 0:
-                    density_ref[:, cells] = new
-                else:
-                    velocity_ref[n - 1, :, cells] = new
-        return carry
-
-    arrived(high + front)
-    lax.fori_loop(0, middle - 1, last_body, 0)
+    def write(part):
+        width = middle * halves * size_z
+        cells = pl.ds(part * width, width)
+        copy = pltpu.make_async_copy(
+            fields.at[:, :, cells], fields_ref.at[:, :, cells], write_sem.at[part]
+        )
+        copy.start()
+        return copy
+
+    arrived(front)
+    last_pass(1, middle - 1)
+    arrived(high)
+    last_pass(0, 1)
     arrived(back)
-    lax.fori_loop(middle - 1, middle, last_body, 0)
+    last_pass(middle - 1, middle)
     early = migrate(0)
-    lax.fori_loop(middle, size_x - 1, last_body, 0)
+    written = [write(0)]
+    last_pass(middle, size_x - 1)
     arrived(low)
-    lax.fori_loop(size_x - 1, size_x, last_body, 0)
+    last_pass(size_x - 1, size_x)
     late = migrate(1)
-    arrived(early)
-    lax.fori_loop(0, middle, place_body, 0)
-    arrived(late)
-    lax.fori_loop(middle, size_x, place_body, 0)
+    written.append(write(1))
     for copy in sent + early + late:
         copy.wait_send()
+    arrived(early + late)
+    for copy in written:
+        copy.wait()
+
+
+def crossings(slot_ref, curve, blocks, sub):
+    home = jnp.full(sub.shape, slot_ref[0] // blocks, jnp.int32)
+    for n in range(1, blocks):
+        home = jnp.where(sub == n, slot_ref[n] // blocks, home)
+    return home == curve + 1, home == curve - 1
+
+
+def place_kernel(slot_ref, fields, come_prev, come_next, density_ref, velocity_ref):
+    _, tiles, width = come_prev.shape
+    blocks = fields.shape[1]
+    tile = (blocks, width)
+    curve = lax.axis_index("bx") * lax.axis_size("by") + lax.axis_index("by")
+    sub = lax.broadcasted_iota(jnp.int32, tile, 0)
+    to_next, to_prev = crossings(slot_ref, curve, blocks, sub)
+    for n in range(4):
+        for at in range(tiles):
+            cells = pl.ds(at * width, width)
+            up = jnp.broadcast_to(come_prev[n, pl.ds(at, 1), :], tile)
+            down = jnp.broadcast_to(come_next[n, pl.ds(at, 1), :], tile)
+            new = jnp.where(to_prev, up, jnp.where(to_next, down, fields[n, :, cells]))
+            if n == 0:
+                density_ref[:, cells] = new
+            else:
+                velocity_ref[n - 1, :, cells] = new
 
 
 def on_device(populations, block_level, new_slot):
@@ -400,40 +446,48 @@
     cells = size_x * size_y * size_z // blocks
     tiles = cells // size_z
     padded = pltpu.VMEM((3, 3, 3, size_x + 2, size_y + 2 * PAD, size_z), jnp.float32)
-    moving = pltpu.VMEM((4, tiles, size_z), jnp.float32)
-    return pl.pallas_call(
+    moving = (4, tiles, size_z)
+    fields, come_prev, come_next = pl.pallas_call(
         functools.partial(kernel, sizes),
         out_shape=(
-            jax.ShapeDtypeStruct((blocks, cells), jnp.float32),
-            jax.ShapeDtypeStruct((3, blocks, cells), jnp.float32),
+            jax.ShapeDtypeStruct((4, blocks, cells), jnp.float32),
+            jax.ShapeDtypeStruct(moving, jnp.float32),
+            jax.ShapeDtypeStruct(moving, jnp.float32),
         ),
-        in_specs=[
-            pl.BlockSpec(memory_space=pltpu.HBM),
-            pl.BlockSpec(memory_space=pltpu.HBM),
-            pl.BlockSpec(memory_space=pltpu.HBM),
-        ],
-        out_specs=[pl.BlockSpec(memory_space=pltpu.VMEM)] * 2,
+        in_specs=[pl.BlockSpec(memory_space=pltpu.HBM)] * 3,
+        out_specs=[pl.BlockSpec(memory_space=pltpu.HBM)] * 3,
         scratch_shapes=[
             pltpu.SMEM(block_level.shape, jnp.int32),
             pltpu.SMEM(new_slot.shape, jnp.int32),
             pltpu.VMEM(populations.shape, jnp.float32),
             padded,
             padded,
-            pltpu.VMEM((3, size_y // 8, 27, 8, size_z), jnp.float32),
-            moving,
-            moving,
-            moving,
-            moving,
+            pltpu.VMEM((27, 8, size_z), jnp.float32),
+            pltpu.VMEM(moving, jnp.float32),
+            pltpu.VMEM(moving, jnp.float32),
+            pltpu.VMEM((4, blocks, cells), jnp.float32),
             pltpu.SemaphoreType.DMA((6,)),
             pltpu.SemaphoreType.DMA((2, 10)),
             pltpu.SemaphoreType.DMA((2, 10)),
             pltpu.SemaphoreType.DMA((2, 2)),
             pltpu.SemaphoreType.DMA((2, 2)),
+            pltpu.SemaphoreType.DMA((2,)),
         ],
         compiler_params=pltpu.CompilerParams(
             collective_id=0, has_side_effects=True, vmem_limit_bytes=60 * 1024 * 1024
         ),
     )(block_level, new_slot, populations)
+    in_vmem = pl.BlockSpec(memory_space=pltpu.VMEM)
+    return pl.pallas_call(
+        place_kernel,
+        out_shape=(
+            jax.ShapeDtypeStruct((blocks, cells), jnp.float32),
+            jax.ShapeDtypeStruct((3, blocks, cells), jnp.float32),
+        ),
+        in_specs=[pl.BlockSpec(memory_space=pltpu.SMEM), in_vmem, in_vmem, in_vmem],
+        out_specs=[in_vmem, in_vmem],
+        compiler_params=pltpu.CompilerParams(vmem_limit_bytes=60 * 1024 * 1024),
+    )(new_slot, fields, come_prev, come_next)
 
 
 def solution(mesh):

time: 31.7 us -> 28.4 us (0.90)
  local copies, waits for them, and re-layouts: 3.33 us -> 0 us
    unnamed x2 -> x0, local copies, waits for them, and re-layouts: 3.33 us -> none
    pallas_call x0 -> x1, Pallas kernels: none -> 1.95 us  [on_device(): pl.pallas_call(place_kernel, out_shape=(jax.ShapeDtypeStruct((blocks, cel...]
    pallas_call x1, Pallas kernels: 27.6 us -> 25.7 us  [on_device(): pl.pallas_call(functools.partial(kernel, sizes), out_shape=(jax.ShapeDtyp...]
where the time goes in v2:
time: 28.4 us; the launch traced here: 28.3 us
  Pallas kernels  27.6 us (97%)
  between operations  0.64 us (2%)
    pallas_call x1, Pallas kernels, on_device(): pl.pallas_call(functools.partial(kernel, sizes), out_shape=(jax.ShapeDtyp...  25.7 us
    pallas_call x1, Pallas kernels, on_device(): pl.pallas_call(place_kernel, out_shape=(jax.ShapeDtypeStruct((blocks, cel...  1.95 us

profile of v2, /device:TPU:0, one launch (start us, length us, event | category | flops | bytes accessed | tf_op | source)
XLA Modules:
  0.0 28.3 jit_solution(13868603798781093399)
XLA Ops:
  0.6 25.7 %shard_map.50 = (f32[4,8,4096]{2,1,0:T(8,128)}, f32[4,32,128]{2,1,0:T(8,128)}, f32[4,32,128]{2,1,0:T(8,128)}) custom-call(s32[256]{0:T(256)} %level_hbm.1, s32[8]{0:T(128)} %slot_ref.1, f32[27,16,16,128]{3,2,1,0:T(8,128)} %pop_ref.1), custom_call_target="tpu_custom_call" | custom-call | tf_op jit(solution)/shard_map/pallas_call | solution.py:450
  26.3 2.0 %shard_map.51 = (f32[8,4096]{1,0:T(8,128)}, f32[3,8,4096]{2,1,0:T(8,128)}) custom-call(s32[8]{0:T(128)} %slot_ref.1, f32[4,8,4096]{2,1,0:T(8,128)} %get-tuple-element.5.fields, f32[4,32,128]{2,1,0:T(8,128)} %get-tuple-element.6.come_prev, f32[4,32,128]{2,1,0:T(8,128)} %get-tuple-element.7.come_next), custom_call_target="tpu_custom_call" | custom-call | tf_op jit(solution)/shard_map/pallas_call | solution.py:481

commit v3 on v2

--- a/solution.py
+++ b/solution.py
@@ -44,7 +44,7 @@
     return rho, momentum, stress
 
 
-def relax(f, base_time, inactive, kind_of, factor_of):
+def settle(f, base_time, inactive):
     rho, (jx, jy, jz), (ends, whole, diff, along_x, y_low, y_high, diff_x) = first_moments(f)
     pxx = along_x[0] + along_x[2]
     pyy = y_low + y_high
@@ -64,35 +64,38 @@
     pxz = pxz - jx * uz
     pyz = pyz - jy * uz
     off = pxy * pxy + pxz * pxz + pyz * pyz
-    norm = jnp.sqrt(pxx * pxx + pyy * pyy + pzz * pzz + (off + off))
-    tau = 0.5 * (base_time + jnp.sqrt(base_time * base_time + SMAGORINSKY * norm * inv))
-    keep = 1.0 - 1.0 / tau
+    square = pxx * pxx + pyy * pyy + pzz * pzz + (off + off)
+    norm = square * lax.rsqrt(jnp.maximum(square, 1e-37))
+    under = base_time * base_time + SMAGORINSKY * norm * inv
+    keep = 1.0 - 2.0 / (base_time + under * lax.rsqrt(under))
     if inactive is not None:
         keep = jnp.where(inactive, 1.0, keep)
+    return rho, ux, uy, uz, keep
+
+
+def outgoing(settled, field_of, kind_of, factor_of, store):
+    rho, ux, uy, uz, keep = settled
     rest = 1.0 - 1.5 * (ux * ux + uy * uy + uz * uz)
     scaled = [rho * w for w in WEIGHTS]
     rests = [s * rest for s in scaled]
     squares = [s * 4.5 for s in scaled]
     linear = [s * 3.0 for s in scaled]
-    out = {}
     keeps = {(1, 1, 1): keep}
 
     def emit(d, balance):
         kind = kind_of(d)
         if kind not in keeps:
             keeps[kind] = keep * factor_of(kind)
-        out[d] = balance + (f[d] - balance) * keeps[kind]
+        store(d, balance + (field_of(d) - balance) * keeps[kind])
 
     emit((1, 1, 1), rests[0])
-    plane = {}
-    for a in (1, 2):
-        for b in range(3):
-            if a == 1 and b == 1:
-                plane[a, b] = None
-            elif a == 1:
-                plane[a, b] = uy if b == 2 else -uy
-            else:
-                plane[a, b] = ux if b == 1 else (ux + uy if b == 2 else ux - uy)
+    plane = {
+        (1, 1): None,
+        (1, 2): uy,
+        (2, 0): ux - uy,
+        (2, 1): ux,
+        (2, 2): ux + uy,
+    }
     for d in HALF:
         a, b, e = d
         level = sum(part != 1 for part in d)
@@ -107,7 +110,6 @@
         odd = linear[level] * proj
         emit(d, even + odd)
         emit(opposite(d), even - odd)
-    return out
 
 
 def swap_chunks(value, sub, chunk):
@@ -158,8 +160,8 @@
     near_x = [lax.rem(index_x + count_x + a - 1, count_x) for a in range(3)]
     near_y = [lax.rem(index_y + count_y + b - 1, count_y) for b in range(3)]
 
-    middle = size_x // 2
-    pieces = ((0, 1), (size_x - 1, size_x), (1, middle), (middle, size_x - 1))
+    cuts = (0, size_x // 2 - 1, size_x // 2 + 3, size_x)
+    pieces = ((0, 1), (size_x - 1, size_x), (1, cuts[1]), (cuts[1], cuts[2]), (cuts[2], size_x - 1))
     loads = []
     for n, (low, high) in enumerate(pieces):
         piece = pl.ds(low, high - low)
@@ -223,19 +225,12 @@
     def factor_of(kind):
         return factors[9 * kind[0] + 3 * kind[1] + kind[2]]
 
-    def put(target, x, half, out):
-        for d in DIRECTIONS:
-            target[d[0], d[1], d[2], x + 1, pl.ds(PAD + 8 * half, 8), :] = out[d]
-
     def row_at(source, x, half, d):
         a, b, e = d
         return source[a, b, e, x + 2 - a, pl.ds(PAD + 8 * half + 1 - b, 8), :]
 
     def along_z(value, e):
         return pltpu.roll(value, (e - 1) % size_z, 1) if e != 1 else value
-
-    def pulled(source, x, half):
-        return {d: along_z(row_at(source, x, half, d), d[2]) for d in DIRECTIONS}
 
     def pulled_moments(source, x, half):
         parts = []
@@ -249,10 +244,8 @@
         rho, jx, jy = (parts[0][n] + parts[1][n] + parts[2][n] for n in range(3))
         return rho, (jx, jy, parts[2][0] - parts[0][0])
 
-    def held_at(x, half):
-        return {
-            (a, b, e): held[9 * a + 3 * b + e, x, pl.ds(8 * half, 8), :] for a, b, e in DIRECTIONS
-        }
+    def held_row(x, half, d):
+        return held[9 * d[0] + 3 * d[1] + d[2], x, pl.ds(8 * half, 8), :]
 
     def send(buffer, turn, side, part=0):
         a, b = side
@@ -262,7 +255,7 @@
         there_y = {0: PAD + size_y, 2: PAD - 1}
         dirs_a = pl.ds(a, 1) if a != 1 else pl.ds(0, 3)
         dirs_b = pl.ds(b, 1) if b != 1 else pl.ds(0, 3)
-        along = pl.ds(1 + part * middle, middle)
+        along = pl.ds(1 + cuts[part], cuts[part + 1] - cuts[part])
         from_x = pl.ds(here_x[a], 1) if a != 1 else along
         into_x = pl.ds(there_x[a], 1) if a != 1 else along
         from_y = pl.ds(here_y[b], 1) if b != 1 else pl.ds(PAD, size_y)
@@ -292,79 +285,104 @@
         for copy in copies:
             copy.wait_recv()
 
-    def first_pass(begin, end, edge=1):
-        def body(x, carry):
-            for half in range(halves):
-                out = relax(held_at(x, half), base_time, coarse, kinds(edge, half), factor_of)
-                put(first, x, half, out)
+    def planes(work, begin, end):
+        def body(n, carry):
+            x = begin + 2 * n
+            work([(x, 1), (x + 1, 1)])
             return carry
 
-        lax.fori_loop(begin, end, body, 0)
-
-    def second_pass(begin, end, edge=1):
-        def body(x, carry):
-            for half in range(halves):
-                kept, moved = held_at(x, half), pulled(first, x, half)
-                f = {d: jnp.where(fine, moved[d], kept[d]) for d in DIRECTIONS}
-                put(second, x, half, relax(f, base_time, None, kinds(edge, half), factor_of))
-            return carry
-
-        lax.fori_loop(begin, end, body, 0)
+        lax.fori_loop(0, (end - begin) // 2, body, 0)
+
+    edges = [(0, 0), (size_x - 1, 2)]
+
+    def emit_tiles(target, tiles, settled):
+        for (x, half, edge), values in zip(tiles, settled):
+
+            def field_of(d, x=x, half=half):
+                return held_row(x, half, d)
+
+            def store(d, value, x=x, half=half):
+                target[d[0], d[1], d[2], x + 1, pl.ds(PAD + 8 * half, 8), :] = value
+
+            outgoing(values, field_of, kinds(edge, half), factor_of, store)
+
+    def first_pass(picked):
+        tiles = [(x, half, edge) for x, edge in picked for half in range(halves)]
+        settled = []
+        for x, half, _ in tiles:
+            f = {d: held_row(x, half, d) for d in DIRECTIONS}
+            settled.append(settle(f, base_time, coarse))
+        emit_tiles(first, tiles, settled)
+
+    def second_pass(picked):
+        tiles = [(x, half, edge) for x, edge in picked for half in range(halves)]
+        settled = []
+        for x, half, _ in tiles:
+            f = {}
+            for d in DIRECTIONS:
+                moved = along_z(row_at(first, x, half, d), d[2])
+                f[d] = jnp.where(fine, moved, held_row(x, half, d))
+                held[9 * d[0] + 3 * d[1] + d[2], x, pl.ds(8 * half, 8), :] = f[d]
+            settled.append(settle(f, base_time, None))
+        emit_tiles(second, tiles, settled)
 
     loads[0].wait()
-    first_pass(0, 1, 0)
+    loads[1].wait()
+    first_pass(edges)
     pl.semaphore_wait(barrier, len(SIDES))
     low = send_low(first, 0)
-    loads[1].wait()
-    first_pass(size_x - 1, size_x, 2)
     high = send_high(first, 0)
-    loads[2].wait()
-    first_pass(1, middle)
-    front = send_part(first, 0, 0)
-    loads[3].wait()
-    first_pass(middle, size_x - 1)
-    back = send_part(first, 0, 1)
-    sent = low + high + front + back
-
-    arrived(high + front)
-    second_pass(0, 1, 0)
-    next_low = send_low(second, 1)
-    second_pass(1, middle - 1)
-    arrived(low + back)
-    second_pass(size_x - 1, size_x, 2)
+    parts = []
+    begin = 1
+    for part in range(3):
+        end = min(cuts[part + 1], size_x - 1)
+        loads[2 + part].wait()
+        planes(first_pass, begin, end)
+        parts.append(send_part(first, 0, part))
+        begin = end
+    sent = low + high + parts[0] + parts[1] + parts[2]
+
+    arrived(parts[0])
+    planes(second_pass, 1, cuts[1] - 2)
+    arrived(parts[1])
+    planes(second_pass, cuts[1] - 2, cuts[2] - 2)
+    arrived(parts[2] + low + high)
+    second_pass(edges)
+    low = send_low(second, 1)
     high = send_high(second, 1)
-    low = next_low
-    second_pass(middle - 1, middle)
-    front = send_part(second, 1, 0)
-    second_pass(middle, size_x - 1)
-    back = send_part(second, 1, 1)
-    sent = sent + low + high + front + back
-
-    to_next, to_prev = crossings(slot_ref, index_x * count_y + index_y, blocks, sub)
-
-    def last_pass(begin, end):
-        def body(x, carry):
+    parts = [send_part(second, 1, 0)]
+    planes(second_pass, cuts[2] - 2, cuts[2])
+    parts.append(send_part(second, 1, 1))
+    planes(second_pass, cuts[2], size_x - 1)
+    parts.append(send_part(second, 1, 2))
+    sent = sent + low + high + parts[0] + parts[1] + parts[2]
+
+    curve = index_x * count_y + index_y
+    next_row = jnp.int32(0)
+    prev_row = jnp.int32(0)
+    for n in range(blocks):
+        next_row = jnp.where(slot_ref[n] // blocks == curve + 1, n, next_row)
+        prev_row = jnp.where(slot_ref[n] // blocks == curve - 1, n, prev_row)
+
+    def last_pass(picked):
+        for x, _ in picked:
             for half in range(halves):
                 rho, momentum = pulled_moments(second, x, half)
                 inv = 1.0 / rho
-                at = x * halves + half
-                cells = pl.ds(pl.multiple_of(at * size_z, size_z), size_z)
+                row = lax.rem(x + size_x - 1, size_x) * halves + half
                 for n, field in enumerate([rho] + [part * inv for part in momentum]):
-                    field = swap_chunks(field, sub, chunk)
-                    fields[n, :, cells] = field
-                    for mask, buffer in ((to_next, leave_next), (to_prev, leave_prev)):
-                        buffer[n, pl.ds(at, 1), :] = jnp.sum(
-                            jnp.where(mask, field, 0.0), axis=0, keepdims=True
-                        )
-            return carry
-
-        lax.fori_loop(begin, end, body, 0)
+                    fields[n, row] = swap_chunks(field, sub, chunk)
+                for n in range(4):
+                    leave_next[n, pl.ds(row, 1), :] = fields[n, row, pl.ds(next_row, 1), :]
+                    leave_prev[n, pl.ds(row, 1), :] = fields[n, row, pl.ds(prev_row, 1), :]
 
     after_x = lax.rem(index_x + (index_y + 1) // count_y, count_x)
     before_x = lax.rem(index_x + count_x - (count_y - index_y) // count_y, count_x)
 
+    marks = (0, cuts[2] - 1, size_x)
+
     def migrate(part):
-        rows = pl.ds(part * middle * halves, middle * halves)
+        rows = pl.ds(marks[part] * halves, (marks[part + 1] - marks[part]) * halves)
         copies = []
         for n, (source, target, device) in enumerate(
             (
@@ -385,25 +403,24 @@
         return copies
 
     def write(part):
-        width = middle * halves * size_z
-        cells = pl.ds(part * width, width)
+        rows = pl.ds(marks[part] * halves, (marks[part + 1] - marks[part]) * halves)
         copy = pltpu.make_async_copy(
-            fields.at[:, :, cells], fields_ref.at[:, :, cells], write_sem.at[part]
+            fields.at[:, rows], fields_ref.at[:, rows], write_sem.at[part]
         )
         copy.start()
         return copy
 
-    arrived(front)
-    last_pass(1, middle - 1)
-    arrived(high)
-    last_pass(0, 1)
-    arrived(back)
-    last_pass(middle - 1, middle)
+    arrived(parts[0])
+    planes(last_pass, 1, cuts[1] - 2)
+    arrived(parts[1])
+    planes(last_pass, cuts[1] - 2, cuts[2] - 2)
+    arrived(parts[2])
+    planes(last_pass, cuts[2] - 2, cuts[2])
     early = migrate(0)
     written = [write(0)]
-    last_pass(middle, size_x - 1)
-    arrived(low)
-    last_pass(size_x - 1, size_x)
+    planes(last_pass, cuts[2], size_x - 1)
+    arrived(low + high)
+    last_pass(edges)
     late = migrate(1)
     written.append(write(1))
     for copy in sent + early + late:
@@ -420,9 +437,9 @@
     return home == curve + 1, home == curve - 1
 
 
-def place_kernel(slot_ref, fields, come_prev, come_next, density_ref, velocity_ref):
+def place_kernel(first_tiles, slot_ref, fields, come_prev, come_next, density_ref, velocity_ref):
     _, tiles, width = come_prev.shape
-    blocks = fields.shape[1]
+    blocks = fields.shape[2]
     tile = (blocks, width)
     curve = lax.axis_index("bx") * lax.axis_size("by") + lax.axis_index("by")
     sub = lax.broadcasted_iota(jnp.int32, tile, 0)
@@ -430,9 +447,10 @@
     for n in range(4):
         for at in range(tiles):
             cells = pl.ds(at * width, width)
-            up = jnp.broadcast_to(come_prev[n, pl.ds(at, 1), :], tile)
-            down = jnp.broadcast_to(come_next[n, pl.ds(at, 1), :], tile)
-            new = jnp.where(to_prev, up, jnp.where(to_next, down, fields[n, :, cells]))
+            row = (at + tiles - first_tiles) % tiles
+            up = jnp.broadcast_to(come_prev[n, pl.ds(row, 1), :], tile)
+            down = jnp.broadcast_to(come_next[n, pl.ds(row, 1), :], tile)
+            new = jnp.where(to_prev, up, jnp.where(to_next, down, fields[n, row]))
             if n == 0:
                 density_ref[:, cells] = new
             else:
@@ -450,7 +468,7 @@
     fields, come_prev, come_next = pl.pallas_call(
         functools.partial(kernel, sizes),
         out_shape=(
-            jax.ShapeDtypeStruct((4, blocks, cells), jnp.float32),
+            jax.ShapeDtypeStruct((4, tiles, blocks, size_z), jnp.float32),
             jax.ShapeDtypeStruct(moving, jnp.float32),
             jax.ShapeDtypeStruct(moving, jnp.float32),
         ),
@@ -465,10 +483,10 @@
             pltpu.VMEM((27, 8, size_z), jnp.float32),
             pltpu.VMEM(moving, jnp.float32),
             pltpu.VMEM(moving, jnp.float32),
-            pltpu.VMEM((4, blocks, cells), jnp.float32),
-            pltpu.SemaphoreType.DMA((6,)),
-            pltpu.SemaphoreType.DMA((2, 10)),
-            pltpu.SemaphoreType.DMA((2, 10)),
+            pltpu.VMEM((4, tiles, blocks, size_z), jnp.float32),
+            pltpu.SemaphoreType.DMA((7,)),
+            pltpu.SemaphoreType.DMA((2, 12)),
+            pltpu.SemaphoreType.DMA((2, 12)),
             pltpu.SemaphoreType.DMA((2, 2)),
             pltpu.SemaphoreType.DMA((2, 2)),
             pltpu.SemaphoreType.DMA((2,)),
@@ -479,7 +497,7 @@
     )(block_level, new_slot, populations)
     in_vmem = pl.BlockSpec(memory_space=pltpu.VMEM)
     return pl.pallas_call(
-        place_kernel,
+        functools.partial(place_kernel, size_y // 8),
         out_shape=(
             jax.ShapeDtypeStruct((blocks, cells), jnp.float32),
             jax.ShapeDtypeStruct((3, blocks, cells), jnp.float32),

time: 28.4 us -> 25.3 us (0.89)
  Pallas kernels: 27.6 us -> 24.5 us
    pallas_call x1, Pallas kernels: 25.7 us -> 22.6 us  [on_device(): pl.pallas_call(functools.partial(kernel, sizes), out_shape=(jax.ShapeDtyp...]
where the time goes in v3:
time: 25.3 us; the launch traced here: 25.1 us
  Pallas kernels  24.5 us (97%)
  between operations  0.64 us (3%)
    pallas_call x1, Pallas kernels, on_device(): pl.pallas_call(functools.partial(kernel, sizes), out_shape=(jax.ShapeDtyp...  22.6 us
    pallas_call x1, Pallas kernels, on_device(): pl.pallas_call(functools.partial(place_kernel, size_y // 8), out_shape=(j...  1.95 us

profile of v3, /device:TPU:0, one launch (start us, length us, event | category | flops | bytes accessed | tf_op | source)
XLA Modules:
  0.0 25.1 jit_solution(10381909173170015056)
XLA Ops:
  0.6 22.6 %shard_map.50 = (f32[4,32,8,128]{3,2,1,0:T(8,128)}, f32[4,32,128]{2,1,0:T(8,128)}, f32[4,32,128]{2,1,0:T(8,128)}) custom-call(s32[256]{0:T(256)} %level_hbm.1, s32[8]{0:T(128)} %slot_ref.1, f32[27,16,16,128]{3,2,1,0:T(8,128)} %pop_ref.1), custom_call_target="tpu_custom_call" | custom-call | tf_op jit(solution)/shard_map/pallas_call | solution.py:468
  23.2 2.0 %shard_map.51 = (f32[8,4096]{1,0:T(8,128)}, f32[3,8,4096]{2,1,0:T(8,128)}) custom-call(s32[8]{0:T(128)} %slot_ref.1, f32[4,32,8,128]{3,2,1,0:T(8,128)} %get-tuple-element.5.fields, f32[4,32,128]{2,1,0:T(8,128)} %get-tuple-element.6.come_prev, f32[4,32,128]{2,1,0:T(8,128)} %get-tuple-element.7.come_next), custom_call_target="tpu_custom_call" | custom-call | tf_op jit(solution)/shard_map/pallas_call | solution.py:499

commit v4 on v3

--- a/solution.py
+++ b/solution.py
@@ -112,20 +112,9 @@
         emit(opposite(d), even - odd)
 
 
-def swap_chunks(value, sub, chunk):
-    lanes = value.shape[1]
-    width = lanes // 8
-    for k in (4, 2, 1):
-        sub_bit = (sub & k) != 0
-        chunk_bit = (chunk & k) != 0
-        down = pltpu.roll(pltpu.roll(value, k, 0), lanes - width * k, 1)
-        if k == 4:
-            value = jnp.where(sub_bit != chunk_bit, down, value)
-        else:
-            up = pltpu.roll(pltpu.roll(value, 8 - k, 0), width * k, 1)
-            value = jnp.where(
-                sub_bit & ~chunk_bit, down, jnp.where(~sub_bit & chunk_bit, up, value)
-            )
+def swap_chunks(value, indices):
+    for axis, index in indices:
+        value = jnp.take_along_axis(value, index, axis=axis, mode="promise_in_bounds")
     return value
 
 
@@ -357,6 +346,12 @@
     parts.append(send_part(second, 1, 2))
     sent = sent + low + high + parts[0] + parts[1] + parts[2]
 
+    width = size_z // blocks
+    swaps = (
+        (1, (lane + sub * width) % size_z),
+        (0, (sub + 8 - chunk) % 8),
+        (1, ((sub + 8 - chunk) % 8) * width + lane % width),
+    )
     curve = index_x * count_y + index_y
     next_row = jnp.int32(0)
     prev_row = jnp.int32(0)
@@ -371,7 +366,7 @@
                 inv = 1.0 / rho
                 row = lax.rem(x + size_x - 1, size_x) * halves + half
                 for n, field in enumerate([rho] + [part * inv for part in momentum]):
-                    fields[n, row] = swap_chunks(field, sub, chunk)
+                    fields[n, row] = swap_chunks(field, swaps)
                 for n in range(4):
                     leave_next[n, pl.ds(row, 1), :] = fields[n, row, pl.ds(next_row, 1), :]
                     leave_prev[n, pl.ds(row, 1), :] = fields[n, row, pl.ds(prev_row, 1), :]
@@ -437,24 +432,53 @@
     return home == curve + 1, home == curve - 1
 
 
-def place_kernel(first_tiles, slot_ref, fields, come_prev, come_next, density_ref, velocity_ref):
+def place_kernel(
+    first_tiles,
+    slot_ref,
+    fields_ref,
+    prev_ref,
+    next_ref,
+    density_ref,
+    velocity_ref,
+    fields,
+    come_prev,
+    come_next,
+    placed,
+    in_sem,
+    out_sem,
+):
+    rows = [
+        pltpu.make_async_copy(prev_ref, come_prev, in_sem.at[4]),
+        pltpu.make_async_copy(next_ref, come_next, in_sem.at[5]),
+    ]
+    loads = [
+        pltpu.make_async_copy(fields_ref.at[n], fields.at[n], in_sem.at[n]) for n in range(4)
+    ]
+    for copy in rows + loads:
+        copy.start()
     _, tiles, width = come_prev.shape
     blocks = fields.shape[2]
     tile = (blocks, width)
     curve = lax.axis_index("bx") * lax.axis_size("by") + lax.axis_index("by")
     sub = lax.broadcasted_iota(jnp.int32, tile, 0)
     to_next, to_prev = crossings(slot_ref, curve, blocks, sub)
+    for copy in rows:
+        copy.wait()
+    stores = []
     for n in range(4):
+        loads[n].wait()
         for at in range(tiles):
-            cells = pl.ds(at * width, width)
             row = (at + tiles - first_tiles) % tiles
             up = jnp.broadcast_to(come_prev[n, pl.ds(row, 1), :], tile)
             down = jnp.broadcast_to(come_next[n, pl.ds(row, 1), :], tile)
             new = jnp.where(to_prev, up, jnp.where(to_next, down, fields[n, row]))
-            if n == 0:
-                density_ref[:, cells] = new
-            else:
-                velocity_ref[n - 1, :, cells] = new
+            placed[n, :, pl.ds(at * width, width)] = new
+        target = density_ref if n == 0 else velocity_ref.at[n - 1]
+        store = pltpu.make_async_copy(placed.at[n], target, out_sem.at[n])
+        store.start()
+        stores.append(store)
+    for store in stores:
+        store.wait()
 
 
 def on_device(populations, block_level, new_slot):
@@ -495,15 +519,23 @@
             collective_id=0, has_side_effects=True, vmem_limit_bytes=60 * 1024 * 1024
         ),
     )(block_level, new_slot, populations)
-    in_vmem = pl.BlockSpec(memory_space=pltpu.VMEM)
+    in_hbm = pl.BlockSpec(memory_space=pltpu.HBM)
     return pl.pallas_call(
         functools.partial(place_kernel, size_y // 8),
         out_shape=(
             jax.ShapeDtypeStruct((blocks, cells), jnp.float32),
             jax.ShapeDtypeStruct((3, blocks, cells), jnp.float32),
         ),
-        in_specs=[pl.BlockSpec(memory_space=pltpu.SMEM), in_vmem, in_vmem, in_vmem],
-        out_specs=[in_vmem, in_vmem],
+        in_specs=[pl.BlockSpec(memory_space=pltpu.SMEM), in_hbm, in_hbm, in_hbm],
+        out_specs=[in_hbm, in_hbm],
+        scratch_shapes=[
+            pltpu.VMEM((4, tiles, blocks, size_z), jnp.float32),
+            pltpu.VMEM(moving, jnp.float32),
+            pltpu.VMEM(moving, jnp.float32),
+            pltpu.VMEM((4, blocks, cells), jnp.float32),
+            pltpu.SemaphoreType.DMA((6,)),
+            pltpu.SemaphoreType.DMA((4,)),
+        ],
         compiler_params=pltpu.CompilerParams(vmem_limit_bytes=60 * 1024 * 1024),
     )(new_slot, fields, come_prev, come_next)
 

time: 25.3 us -> 25.4 us (level)
    pallas_call x1, Pallas kernels: 1.95 us -> 2.6 us  [on_device(): pl.pallas_call(functools.partial(place_kernel, size_y // 8), out_shape=(j...]
    pallas_call x1, Pallas kernels: 22.6 us -> 22 us  [on_device(): pl.pallas_call(functools.partial(kernel, sizes), out_shape=(jax.ShapeDtyp...]
where the time goes in v4:
time: 25.4 us; the launch traced here: 25.2 us
  Pallas kernels  24.6 us (97%)
  between operations  0.64 us (3%)
    pallas_call x1, Pallas kernels, on_device(): pl.pallas_call(functools.partial(kernel, sizes), out_shape=(jax.ShapeDtyp...  22 us
    pallas_call x1, Pallas kernels, on_device(): pl.pallas_call(functools.partial(place_kernel, size_y // 8), out_shape=(j...  2.6 us

profile of v4, /device:TPU:0, one launch (start us, length us, event | category | flops | bytes accessed | tf_op | source)
XLA Modules:
  0.0 25.2 jit_solution(6256817716873585608)
XLA Ops:
  0.6 22.0 %shard_map.50 = (f32[4,32,8,128]{3,2,1,0:T(8,128)}, f32[4,32,128]{2,1,0:T(8,128)}, f32[4,32,128]{2,1,0:T(8,128)}) custom-call(s32[256]{0:T(256)} %level_hbm.1, s32[8]{0:T(128)} %slot_ref.1, f32[27,16,16,128]{3,2,1,0:T(8,128)} %pop_ref.1), custom_call_target="tpu_custom_call" | custom-call | tf_op jit(solution)/shard_map/pallas_call | solution.py:492
  22.6 2.6 %shard_map.51 = (f32[8,4096]{1,0:T(8,128)}, f32[3,8,4096]{2,1,0:T(8,128)}) custom-call(s32[8]{0:T(128)} %slot_ref.1, f32[4,32,8,128]{3,2,1,0:T(8,128)} %get-tuple-element.5.fields_ref, f32[4,32,128]{2,1,0:T(8,128)} %get-tuple-element.6.prev_ref, f32[4,32,128]{2,1,0:T(8,128)} %get-tuple-element.7.next_ref), custom_call_target="tpu_custom_call" | custom-call | tf_op jit(solution)/shard_map/pallas_call | solution.py:523

commit v5 on v3

--- a/solution.py
+++ b/solution.py
@@ -112,20 +112,9 @@
         emit(opposite(d), even - odd)
 
 
-def swap_chunks(value, sub, chunk):
-    lanes = value.shape[1]
-    width = lanes // 8
-    for k in (4, 2, 1):
-        sub_bit = (sub & k) != 0
-        chunk_bit = (chunk & k) != 0
-        down = pltpu.roll(pltpu.roll(value, k, 0), lanes - width * k, 1)
-        if k == 4:
-            value = jnp.where(sub_bit != chunk_bit, down, value)
-        else:
-            up = pltpu.roll(pltpu.roll(value, 8 - k, 0), width * k, 1)
-            value = jnp.where(
-                sub_bit & ~chunk_bit, down, jnp.where(~sub_bit & chunk_bit, up, value)
-            )
+def swap_chunks(value, indices):
+    for axis, index in indices:
+        value = jnp.take_along_axis(value, index, axis=axis, mode="promise_in_bounds")
     return value
 
 
@@ -160,8 +149,9 @@
     near_x = [lax.rem(index_x + count_x + a - 1, count_x) for a in range(3)]
     near_y = [lax.rem(index_y + count_y + b - 1, count_y) for b in range(3)]
 
-    cuts = (0, size_x // 2 - 1, size_x // 2 + 3, size_x)
-    pieces = ((0, 1), (size_x - 1, size_x), (1, cuts[1]), (cuts[1], cuts[2]), (cuts[2], size_x - 1))
+    last = size_x - 1
+    cuts = (0, 1, size_x // 2 - 1, size_x // 2 + 3, last, size_x)
+    pieces = ((last, size_x), (1, cuts[2]), (cuts[2], cuts[3]), (0, 1), (cuts[3], last))
     loads = []
     for n, (low, high) in enumerate(pieces):
         piece = pl.ds(low, high - low)
@@ -293,7 +283,8 @@
 
         lax.fori_loop(0, (end - begin) // 2, body, 0)
 
-    edges = [(0, 0), (size_x - 1, 2)]
+    low_plane = [(0, 0)]
+    high_plane = [(last, 2)]
 
     def emit_tiles(target, tiles, settled):
         for (x, half, edge), values in zip(tiles, settled):
@@ -327,36 +318,52 @@
         emit_tiles(second, tiles, settled)
 
     loads[0].wait()
+    first_pass(high_plane)
+    pl.semaphore_wait(barrier, len(SIDES))
+    high = send_high(first, 0)
+    rows = {4: send_part(first, 0, 4)}
     loads[1].wait()
-    first_pass(edges)
-    pl.semaphore_wait(barrier, len(SIDES))
+    planes(first_pass, 1, cuts[2])
+    rows[1] = send_part(first, 0, 1)
+    loads[2].wait()
+    planes(first_pass, cuts[2], cuts[3])
+    rows[2] = send_part(first, 0, 2)
+    loads[3].wait()
+    first_pass(low_plane)
     low = send_low(first, 0)
-    high = send_high(first, 0)
-    parts = []
-    begin = 1
-    for part in range(3):
-        end = min(cuts[part + 1], size_x - 1)
-        loads[2 + part].wait()
-        planes(first_pass, begin, end)
-        parts.append(send_part(first, 0, part))
-        begin = end
-    sent = low + high + parts[0] + parts[1] + parts[2]
-
-    arrived(parts[0])
-    planes(second_pass, 1, cuts[1] - 2)
-    arrived(parts[1])
-    planes(second_pass, cuts[1] - 2, cuts[2] - 2)
-    arrived(parts[2] + low + high)
-    second_pass(edges)
-    low = send_low(second, 1)
+    rows[0] = send_part(first, 0, 0)
+    loads[4].wait()
+    planes(first_pass, cuts[3], last)
+    rows[3] = send_part(first, 0, 3)
+    sent = low + high + sum(rows.values(), [])
+
+    arrived(rows[0] + rows[1])
+    planes(second_pass, 1, cuts[2] - 2)
+    arrived(high)
+    second_pass(low_plane)
+    next_low = send_low(second, 1)
+    next_rows = {0: send_part(second, 1, 0)}
+    arrived(rows[2])
+    planes(second_pass, cuts[2] - 2, cuts[3] - 2)
+    next_rows[1] = send_part(second, 1, 1)
+    arrived(rows[3] + rows[4])
+    planes(second_pass, cuts[3] - 2, cuts[3])
+    next_rows[2] = send_part(second, 1, 2)
+    arrived(low)
+    second_pass(high_plane)
     high = send_high(second, 1)
-    parts = [send_part(second, 1, 0)]
-    planes(second_pass, cuts[2] - 2, cuts[2])
-    parts.append(send_part(second, 1, 1))
-    planes(second_pass, cuts[2], size_x - 1)
-    parts.append(send_part(second, 1, 2))
-    sent = sent + low + high + parts[0] + parts[1] + parts[2]
-
+    next_rows[4] = send_part(second, 1, 4)
+    planes(second_pass, cuts[3], last)
+    next_rows[3] = send_part(second, 1, 3)
+    low, rows = next_low, next_rows
+    sent = sent + low + high + sum(rows.values(), [])
+
+    width = size_z // blocks
+    swaps = (
+        (1, (lane + sub * width) % size_z),
+        (0, (sub + 8 - chunk) % 8),
+        (1, ((sub + 8 - chunk) % 8) * width + lane % width),
+    )
     curve = index_x * count_y + index_y
     next_row = jnp.int32(0)
     prev_row = jnp.int32(0)
@@ -371,7 +378,7 @@
                 inv = 1.0 / rho
                 row = lax.rem(x + size_x - 1, size_x) * halves + half
                 for n, field in enumerate([rho] + [part * inv for part in momentum]):
-                    fields[n, row] = swap_chunks(field, sub, chunk)
+                    fields[n, row] = swap_chunks(field, swaps)
                 for n in range(4):
                     leave_next[n, pl.ds(row, 1), :] = fields[n, row, pl.ds(next_row, 1), :]
                     leave_prev[n, pl.ds(row, 1), :] = fields[n, row, pl.ds(prev_row, 1), :]
@@ -379,7 +386,7 @@
     after_x = lax.rem(index_x + (index_y + 1) // count_y, count_x)
     before_x = lax.rem(index_x + count_x - (count_y - index_y) // count_y, count_x)
 
-    marks = (0, cuts[2] - 1, size_x)
+    marks = (0, last, size_x)
 
     def migrate(part):
         rows = pl.ds(marks[part] * halves, (marks[part + 1] - marks[part]) * halves)
@@ -410,17 +417,18 @@
         copy.start()
         return copy
 
-    arrived(parts[0])
-    planes(last_pass, 1, cuts[1] - 2)
-    arrived(parts[1])
-    planes(last_pass, cuts[1] - 2, cuts[2] - 2)
-    arrived(parts[2])
-    planes(last_pass, cuts[2] - 2, cuts[2])
+    arrived(rows[0] + rows[1])
+    planes(last_pass, 1, cuts[2] - 2)
+    arrived(rows[2])
+    planes(last_pass, cuts[2] - 2, cuts[3] - 2)
+    arrived(rows[3] + rows[4])
+    planes(last_pass, cuts[3] - 2, last)
+    arrived(low)
+    last_pass(high_plane)
     early = migrate(0)
     written = [write(0)]
-    planes(last_pass, cuts[2], size_x - 1)
-    arrived(low + high)
-    last_pass(edges)
+    arrived(high)
+    last_pass(low_plane)
     late = migrate(1)
     written.append(write(1))
     for copy in sent + early + late:
@@ -485,8 +493,8 @@
             pltpu.VMEM(moving, jnp.float32),
             pltpu.VMEM((4, tiles, blocks, size_z), jnp.float32),
             pltpu.SemaphoreType.DMA((7,)),
-            pltpu.SemaphoreType.DMA((2, 12)),
-            pltpu.SemaphoreType.DMA((2, 12)),
+            pltpu.SemaphoreType.DMA((2, 16)),
+            pltpu.SemaphoreType.DMA((2, 16)),
             pltpu.SemaphoreType.DMA((2, 2)),
             pltpu.SemaphoreType.DMA((2, 2)),
             pltpu.SemaphoreType.DMA((2,)),

time: 25.3 us -> 25.3 us (level)
  no operation moved by 1% of the time
where the time goes in v5:
time: 25.3 us; the launch traced here: 25.1 us
  Pallas kernels  24.5 us (97%)
  between operations  0.64 us (3%)
    pallas_call x1, Pallas kernels, on_device(): pl.pallas_call(functools.partial(kernel, sizes), out_shape=(jax.ShapeDtyp...  22.5 us
    pallas_call x1, Pallas kernels, on_device(): pl.pallas_call(functools.partial(place_kernel, size_y // 8), out_shape=(j...  1.95 us

profile of v5, /device:TPU:0, one launch (start us, length us, event | category | flops | bytes accessed | tf_op | source)
XLA Modules:
  0.0 25.1 jit_solution(2676877567703069320)
XLA Ops:
  0.6 22.5 %shard_map.50 = (f32[4,32,8,128]{3,2,1,0:T(8,128)}, f32[4,32,128]{2,1,0:T(8,128)}, f32[4,32,128]{2,1,0:T(8,128)}) custom-call(s32[256]{0:T(256)} %level_hbm.1, s32[8]{0:T(128)} %slot_ref.1, f32[27,16,16,128]{3,2,1,0:T(8,128)} %pop_ref.1), custom_call_target="tpu_custom_call" | custom-call | tf_op jit(solution)/shard_map/pallas_call | solution.py:476
  23.2 2.0 %shard_map.51 = (f32[8,4096]{1,0:T(8,128)}, f32[3,8,4096]{2,1,0:T(8,128)}) custom-call(s32[8]{0:T(128)} %slot_ref.1, f32[4,32,8,128]{3,2,1,0:T(8,128)} %get-tuple-element.5.fields, f32[4,32,128]{2,1,0:T(8,128)} %get-tuple-element.6.come_prev, f32[4,32,128]{2,1,0:T(8,128)} %get-tuple-element.7.come_next), custom_call_target="tpu_custom_call" | custom-call | tf_op jit(solution)/shard_map/pallas_call | solution.py:507

commit v6 on v5

--- a/solution.py
+++ b/solution.py
@@ -150,7 +150,7 @@
     near_y = [lax.rem(index_y + count_y + b - 1, count_y) for b in range(3)]
 
     last = size_x - 1
-    cuts = (0, 1, size_x // 2 - 1, size_x // 2 + 3, last, size_x)
+    cuts = (0, 1, size_x // 2 - 1, size_x // 2 + 3, size_x // 2 + 5, last, size_x)
     pieces = ((last, size_x), (1, cuts[2]), (cuts[2], cuts[3]), (0, 1), (cuts[3], last))
     loads = []
     for n, (low, high) in enumerate(pieces):
@@ -321,7 +321,7 @@
     first_pass(high_plane)
     pl.semaphore_wait(barrier, len(SIDES))
     high = send_high(first, 0)
-    rows = {4: send_part(first, 0, 4)}
+    rows = {5: send_part(first, 0, 5)}
     loads[1].wait()
     planes(first_pass, 1, cuts[2])
     rows[1] = send_part(first, 0, 1)
@@ -333,8 +333,10 @@
     low = send_low(first, 0)
     rows[0] = send_part(first, 0, 0)
     loads[4].wait()
-    planes(first_pass, cuts[3], last)
+    planes(first_pass, cuts[3], cuts[4])
     rows[3] = send_part(first, 0, 3)
+    planes(first_pass, cuts[4], last)
+    rows[4] = send_part(first, 0, 4)
     sent = low + high + sum(rows.values(), [])
 
     arrived(rows[0] + rows[1])
@@ -346,15 +348,17 @@
     arrived(rows[2])
     planes(second_pass, cuts[2] - 2, cuts[3] - 2)
     next_rows[1] = send_part(second, 1, 1)
-    arrived(rows[3] + rows[4])
+    arrived(rows[3])
     planes(second_pass, cuts[3] - 2, cuts[3])
     next_rows[2] = send_part(second, 1, 2)
-    arrived(low)
+    arrived(rows[4] + rows[5] + low)
     second_pass(high_plane)
     high = send_high(second, 1)
+    next_rows[5] = send_part(second, 1, 5)
+    planes(second_pass, cuts[3], cuts[4])
+    next_rows[3] = send_part(second, 1, 3)
+    planes(second_pass, cuts[4], last)
     next_rows[4] = send_part(second, 1, 4)
-    planes(second_pass, cuts[3], last)
-    next_rows[3] = send_part(second, 1, 3)
     low, rows = next_low, next_rows
     sent = sent + low + high + sum(rows.values(), [])
 
@@ -386,7 +390,7 @@
     after_x = lax.rem(index_x + (index_y + 1) // count_y, count_x)
     before_x = lax.rem(index_x + count_x - (count_y - index_y) // count_y, count_x)
 
-    marks = (0, last, size_x)
+    marks = (0, cuts[3] - 1, size_x)
 
     def migrate(part):
         rows = pl.ds(marks[part] * halves, (marks[part + 1] - marks[part]) * halves)
@@ -421,12 +425,14 @@
     planes(last_pass, 1, cuts[2] - 2)
     arrived(rows[2])
     planes(last_pass, cuts[2] - 2, cuts[3] - 2)
-    arrived(rows[3] + rows[4])
-    planes(last_pass, cuts[3] - 2, last)
+    arrived(rows[3])
+    planes(last_pass, cuts[3] - 2, cuts[3])
+    early = migrate(0)
+    written = [write(0)]
+    arrived(rows[4] + rows[5])
+    planes(last_pass, cuts[3], last)
     arrived(low)
     last_pass(high_plane)
-    early = migrate(0)
-    written = [write(0)]
     arrived(high)
     last_pass(low_plane)
     late = migrate(1)
@@ -493,8 +499,8 @@
             pltpu.VMEM(moving, jnp.float32),
             pltpu.VMEM((4, tiles, blocks, size_z), jnp.float32),
             pltpu.SemaphoreType.DMA((7,)),
-            pltpu.SemaphoreType.DMA((2, 16)),
-            pltpu.SemaphoreType.DMA((2, 16)),
+            pltpu.SemaphoreType.DMA((2, 18)),
+            pltpu.SemaphoreType.DMA((2, 18)),
             pltpu.SemaphoreType.DMA((2, 2)),
             pltpu.SemaphoreType.DMA((2, 2)),
             pltpu.SemaphoreType.DMA((2,)),

time: 25.3 us -> 24.9 us (0.984)
  Pallas kernels: 24.5 us -> 24.1 us
    pallas_call x1, Pallas kernels: 22.5 us -> 22.1 us  [on_device(): pl.pallas_call(functools.partial(kernel, sizes), out_shape=(jax.ShapeDtyp...]
where the time goes in v6:
time: 24.9 us; the launch traced here: 24.7 us
  Pallas kernels  24.1 us (97%)
  between operations  0.64 us (3%)
    pallas_call x1, Pallas kernels, on_device(): pl.pallas_call(functools.partial(kernel, sizes), out_shape=(jax.ShapeDtyp...  22.1 us
    pallas_call x1, Pallas kernels, on_device(): pl.pallas_call(functools.partial(place_kernel, size_y // 8), out_shape=(j...  1.95 us

profile of v6, /device:TPU:0, one launch (start us, length us, event | category | flops | bytes accessed | tf_op | source)
XLA Modules:
  0.0 24.7 jit_solution(5112435982524191881)
XLA Ops:
  0.6 22.1 %shard_map.50 = (f32[4,32,8,128]{3,2,1,0:T(8,128)}, f32[4,32,128]{2,1,0:T(8,128)}, f32[4,32,128]{2,1,0:T(8,128)}) custom-call(s32[256]{0:T(256)} %level_hbm.1, s32[8]{0:T(128)} %slot_ref.1, f32[27,16,16,128]{3,2,1,0:T(8,128)} %pop_ref.1), custom_call_target="tpu_custom_call" | custom-call | tf_op jit(solution)/shard_map/pallas_call | solution.py:482
  22.8 2.0 %shard_map.51 = (f32[8,4096]{1,0:T(8,128)}, f32[3,8,4096]{2,1,0:T(8,128)}) custom-call(s32[8]{0:T(128)} %slot_ref.1, f32[4,32,8,128]{3,2,1,0:T(8,128)} %get-tuple-element.5.fields, f32[4,32,128]{2,1,0:T(8,128)} %get-tuple-element.6.come_prev, f32[4,32,128]{2,1,0:T(8,128)} %get-tuple-element.7.come_next), custom_call_target="tpu_custom_call" | custom-call | tf_op jit(solution)/shard_map/pallas_call | solution.py:513
